TPU v7x, 32 devices: a whole 2x2x4 slice. The times are simulated.
32 devices in a mesh: row: 4 (over y, x), col: 8 (over z, core).
Axes of the slice: x: 2, y: 2, z: 4, core: 2. Of those that a mesh axis runs over, the one named last changes fastest.
Arguments:
- matrix: float32 [4096, 4096], P('row', 'col'), may hold values from -8 to 48
- pivots: int32 [2, 128], replicated, may hold values from 256 to 4095, as said below
- lower_inverse: float32 [2, 128, 128], replicated, may hold values from -1 to 1, as said below
Outputs:
- factored: float32 [4096, 4096], P('row', 'col')
Inputs may be any that keep to these rules, and one draw needn't show every extreme that they name: pivots[k, j] is the global row that panel k exchanges with global row k * 128 + j; all 256 entries are distinct. Each lower_inverse[k] is unit lower triangular.
All inputs are finite; a program needn't handle non-finite values.
Results may differ from a plain program's by a relative error of at most 0.0001.
Values sent between devices are 32-bit elements; how exact they have to be, the bound alone decides.
A program may use at most 64 MiB of HBM per device.

v0:
```python
import jax
import jax.numpy as jnp
from jax import lax
from jax.sharding import PartitionSpec as P


def spread(value, axis, source):
    kept = jnp.where(lax.axis_index(axis) == source, value, 0).astype(value.dtype)
    return lax.psum(kept, axis)


def exact_dot(left, right):
    return jnp.dot(left, right, precision=lax.Precision.HIGHEST, preferred_element_type=jnp.float32)


def upper_inverse(upper):
    size = upper.shape[0]
    diag_vals = jnp.diagonal(upper)
    scaled = upper / diag_vals[:, None]
    eye_mat = jnp.eye(size, dtype=jnp.float32)
    power = eye_mat - scaled
    result = eye_mat + power
    reach = 2
    while reach < size:
        power = exact_dot(power, power)
        result = exact_dot(result, eye_mat + power)
        reach = reach * 2
    return result / diag_vals[None, :]


def on_device(matrix, pivots, lower_inverse):
    row_count = lax.axis_size("row")
    col_count = lax.axis_size("col")
    row_index = lax.axis_index("row")
    col_index = lax.axis_index("col")
    local_height, local_width = matrix.shape
    block_size = lower_inverse.shape[1]
    row_block = jnp.arange(local_height, dtype=jnp.int32) // block_size * row_count + row_index
    col_spots = jnp.arange(local_width, dtype=jnp.int32)
    col_block = col_spots // block_size * col_count + col_index
    col_inner = col_spots % block_size
    tri_rows = jnp.arange(block_size, dtype=jnp.int32)[:, None]
    height_spots = jnp.arange(local_height, dtype=jnp.int32)

    def owner_table(panel_num):
        pivot_rows = pivots[panel_num]
        pivot_block = pivot_rows // block_size
        is_owned = pivot_block % row_count == row_index
        local_rows = pivot_block // row_count * block_size + pivot_rows % block_size
        return (is_owned[:, None] & (local_rows[:, None] == height_spots[None, :])).astype(
            jnp.float32
        )

    factor_work = matrix
    for panel_num in range(pivots.shape[0]):
        pick_selector = owner_table(panel_num)
        pick_taken_rows = exact_dot(pick_selector, factor_work)
        pick_first_row = panel_num // row_count * block_size
        pick_is_root = panel_num % row_count == row_index
        pick_top_rows = jnp.where(
            pick_is_root, factor_work[pick_first_row : pick_first_row + block_size], 0.0
        )
        swap_taken_rows = pick_taken_rows
        swap_top_rows = pick_top_rows
        swap_taken_rows, swap_top_rows = lax.psum((swap_taken_rows, swap_top_rows), "row")
        place_factor_work = factor_work
        selector = owner_table(panel_num)
        hit_rows = jnp.sum(selector, axis=0) > 0.5
        placed = exact_dot(selector.T, swap_top_rows)
        place_factor_work = jnp.where(hit_rows[:, None], placed, place_factor_work)
        place_first_row = panel_num // row_count * block_size
        place_is_root = panel_num % row_count == row_index
        current = place_factor_work[place_first_row : place_first_row + block_size]
        factor_work = place_factor_work.at[place_first_row : place_first_row + block_size].set(
            jnp.where(place_is_root, swap_taken_rows, current)
        )
        full_factor_work = factor_work
        upper_factor_work = full_factor_work
        first_row = panel_num // row_count * block_size
        upper_block_rows = upper_factor_work[first_row : first_row + block_size]
        upper_is_root = panel_num % row_count == row_index
        product = exact_dot(lower_inverse[panel_num], upper_block_rows)
        diag_part = jnp.where(tri_rows <= col_inner[None, :], product, 0.0)
        upper_formed = spread(
            jnp.where(
                col_block[None, :] > panel_num,
                product,
                jnp.where(col_block[None, :] == panel_num, diag_part, upper_block_rows),
            ),
            "row",
            panel_num % row_count,
        )
        upper_factor_work = upper_factor_work.at[first_row : first_row + block_size].set(
            jnp.where(upper_is_root, upper_formed, upper_block_rows)
        )
        full_factor_work = upper_factor_work
        diag_first_col = panel_num // col_count * block_size
        lower_factor_work = full_factor_work
        lower_first_col = panel_num // col_count * block_size
        panel_cols = lower_factor_work[:, lower_first_col : lower_first_col + block_size]
        inverse_upper = upper_inverse(upper_formed[:, diag_first_col : diag_first_col + block_size])
        solved = exact_dot(panel_cols, inverse_upper)
        is_root = panel_num % col_count == col_index
        is_below = (row_block > panel_num)[:, None] & is_root
        lower_factor_work = lower_factor_work.at[
            :, lower_first_col : lower_first_col + block_size
        ].set(jnp.where(is_below, solved, panel_cols))
        lower_sent_panel = spread(jnp.where(is_below, solved, 0.0), "col", panel_num % col_count)
        full_factor_work = lower_factor_work
        change = exact_dot(lower_sent_panel, upper_formed)
        live = (row_block > panel_num)[:, None] & (col_block > panel_num)[None, :]
        factor_work = full_factor_work.at[:, 0 : 0 + local_width].set(
            jnp.where(live, full_factor_work - change, full_factor_work)
        )
    return factor_work


def solution(mesh):
    return jax.shard_map(
        on_device,
        mesh=mesh,
        in_specs=(P("row", "col"), P(), P()),
        out_specs=P("row", "col"),
        check_vma=False,
    )
```

profile of v0, /device:TPU:24, one launch (start us, length us, event | category | flops | bytes accessed | tf_op | source)
XLA Modules:
  0.0 347.7 jit_solution(4987288827838978806)
XLA Ops:
  6.5 0.9 fusion.56
  7.4 0.8 fusion.54
  8.2 1.7 slice_select_fusion.3
  9.9 3.2 fusion.7
  13.2 0.2 convert_reduce_fusion
  13.4 46.3 %all-reduce.19.cloned.1.call-done = (f32[128,512]{1,0:T(8,128)}, f32[128,512]{1,0:T(8,128)}) async-done(((f32[128,512]{1,0:T(8,128)}, f32[128,512]{1,0:T(8,128)}), (f32[128,512]{1,0:T(8,128)}, f32[128,512]{1,0:T(8,128)})) %all-reduce.19.cloned.1.call-update) | async-done | bytes 524304 | tf_op jit(solution)/shard_map/psum | solution.py:65
  59.7 2.1 convolution_select_fusion.1
  61.8 1.3 copy-done.3
  63.2 1.2 select_select_fusion.5
  64.4 0.7 compare_reduce_fusion
  65.1 1.6 copy.15
  66.7 0.1 constant_dynamic-update-slice_fusion.1
  66.7 40.7 %all-reduce.9.cloned.1.call-done = f32[128,512]{1,0:T(8,128)} async-done(((f32[128,512]{1,0:T(8,128)}), f32[128,512]{1,0:T(8,128)}) %all-reduce.9.cloned.1.call-update) | async-done | bytes 262160 | tf_op jit(solution)/shard_map/psum | solution.py:9
  107.4 0.9 slice.189
  108.4 1.2 gather_fusion
  109.6 1.2 fusion.47
  110.8 0.2 fusion.62
  111.0 0.2 fusion.63
  111.2 1.1 fusion.22
  112.3 0.2 fusion.23
  112.6 0.2 fusion.64
  112.8 0.2 fusion.24
  113.0 0.2 fusion.65
  113.2 0.2 fusion.25
  113.4 0.2 convolution_add_fusion.1
  113.6 0.2 fusion.26
  113.8 0.2 convolution_divide_fusion.1
  114.1 1.0 select_dynamic-update-slice_fusion.1
  115.1 0.6 fusion.12
  115.7 1.7 select_select_fusion.3
  117.4 0.0 all-reduce.17.cloned.1.call-start
  117.5 54.2 %all-reduce.11.cloned.1.call-done = f32[1024,128]{1,0:T(8,128)} async-done(((f32[1024,128]{1,0:T(8,128)}), f32[1024,128]{1,0:T(8,128)}) %all-reduce.11.cloned.1.call-update) | async-done | bytes 524304 | tf_op jit(solution)/shard_map/psum | solution.py:9
  171.7 3.7 %subtract_select_fusion.1 = f32[1024,512]{1,0:T(8,128)S(1)} fusion(f32[1024,512]{1,0:T(8,128)} %copy-done, f32[1024,128]{1,0:T(8,128)} %all-reduce.11.cloned.1.call-done, f32[128,512]{1,0:T(8,128)S(1)} %copy-done.4, pred[512]{0:T(512)(128)(4,1)S(1)} %broadcast_compare_fusion.3, pred[1024]{0:T(1024)(128)(4,1)S(1)} %fusion.40), kind=kOutput, calls=%fused_computation.3 | convolution fusion | flops 806879232 | bytes 4982272 | tf_op jit(solution)/shard_map/dot_general | solution.py:13
  175.5 0.7 slice_select_fusion.1
  176.2 1.6 fusion.3
  177.8 0.0 all-reduce.13.cloned.1.call-start
  177.9 0.2 convert_reduce_fusion.1
  178.1 46.3 %all-reduce.17.cloned.1.call-done = (f32[128,512]{1,0:T(8,128)}, f32[128,512]{1,0:T(8,128)}) async-done(((f32[128,512]{1,0:T(8,128)}, f32[128,512]{1,0:T(8,128)}), (f32[128,512]{1,0:T(8,128)}, f32[128,512]{1,0:T(8,128)})) %all-reduce.17.cloned.1.call-update) | async-done | bytes 524304 | tf_op jit(solution)/shard_map/psum | solution.py:65
  224.4 2.2 convolution_select_fusion
  226.6 1.3 copy-done.2
  227.9 1.2 select_select_fusion.4
  229.1 0.2 all-reduce.15.cloned.1.call-start
  229.3 1.6 copy.22
  230.9 0.1 constant_dynamic-update-slice_fusion
  231.0 41.2 %all-reduce.13.cloned.1.call-done = f32[128,512]{1,0:T(8,128)} async-done(((f32[128,512]{1,0:T(8,128)}), f32[128,512]{1,0:T(8,128)}) %all-reduce.13.cloned.1.call-update) | async-done | bytes 262160 | tf_op jit(solution)/shard_map/psum | solution.py:9
  272.2 0.9 slice.193
  273.1 1.2 gather_fusion.1
  274.4 1.2 fusion.48
  275.6 0.2 fusion.66
  275.8 0.2 fusion.67
  276.0 1.1 fusion.27
  277.1 0.2 fusion.28
  277.3 0.2 fusion.68
  277.5 0.2 fusion.29
  277.7 0.2 fusion.69
  278.0 0.2 fusion.30
  278.2 0.2 convolution_add_fusion
  278.4 0.2 fusion.31
  278.6 0.2 convolution_divide_fusion
  278.8 1.0 select_dynamic-update-slice_fusion
  279.8 0.6 fusion.10
  280.4 1.7 select_select_fusion.2
  282.2 54.3 %all-reduce.15.cloned.1.call-done = f32[1024,128]{1,0:T(8,128)} async-done(((f32[1024,128]{1,0:T(8,128)}), f32[1024,128]{1,0:T(8,128)}) %all-reduce.15.cloned.1.call-update) | async-done | bytes 524304 | tf_op jit(solution)/shard_map/psum | solution.py:9
  336.5 4.4 %subtract_select_fusion = f32[1024,512]{1,0:T(8,128)} fusion(f32[1024,512]{1,0:T(8,128)S(1)} %get-tuple-element.126, f32[1024,128]{1,0:T(8,128)} %all-reduce.15.cloned.1.call-done, f32[128,512]{1,0:T(8,128)S(1)} %copy-done.5, pred[512]{0:T(512)(128)(4,1)S(1)} %broadcast_compare_fusion.5, pred[1024]{0:T(1024)(128)(4,1)S(1)} %fusion.41), kind=kOutput, calls=%fused_computation.2 | convolution fusion | flops 806879232 | bytes 4982272 | tf_op jit(solution)/shard_map/dot_general | solution.py:13
  (37 shorter events, 0.3 us)
Async XLA Ops:
  6.5 53.2 %copy-start.1 = (f32[1024,512]{1,0:T(8,128)S(1)}, f32[1024,512]{1,0:T(8,128)}, u32[]{:S(2)}) copy-start(f32[1024,512]{1,0:T(8,128)} %param.23) | copy-start | bytes 6291460
  6.5 53.2 %all-reduce.19.cloned.1.call-start = ((), (), s32[]{:S(2)}) async-start(), calls=%async_computation.5 | async-start | bytes 1048576 | tf_op jit(solution)/shard_map/psum | solution.py:65
  13.1 94.3 %all-reduce.9.cloned.1.call-start = ((), (), s32[]{:S(2)}) async-start(), calls=%async_computation | async-start | bytes 524288 | tf_op jit(solution)/shard_map/psum | solution.py:9
  59.7 3.5 copy-start.6
  59.7 3.5 copy-start.8
  61.8 1.3 copy-start.3
  64.4 107.4 %all-reduce.11.cloned.1.call-start = ((), (), s32[]{:S(2)}) async-start(), calls=%async_computation.1 | async-start | bytes 1048576 | tf_op jit(solution)/shard_map/psum | solution.py:9
  107.4 6.6 %copy-start.4 = (f32[128,512]{1,0:T(8,128)S(1)}, f32[128,512]{1,0:T(8,128)}, u32[]{:S(2)}) copy-start(f32[128,512]{1,0:T(8,128)} %all-reduce.9.cloned.1.call-done) | copy-start | bytes 786436
  117.4 54.3 %copy-start = (f32[1024,512]{1,0:T(8,128)}, f32[1024,512]{1,0:T(8,128)S(1)}, u32[]{:S(2)}) copy-start(f32[1024,512]{1,0:T(8,128)S(1)} %get-tuple-element.128) | copy-start | bytes 6291460
  117.4 107.0 %all-reduce.17.cloned.1.call-start = ((), (), s32[]{:S(2)}) async-start(), calls=%async_computation.4 | async-start | bytes 1048576 | tf_op jit(solution)/shard_map/psum | solution.py:65
  177.8 94.4 %all-reduce.13.cloned.1.call-start = ((), (), s32[]{:S(2)}) async-start(), calls=%async_computation.2 | async-start | bytes 524288 | tf_op jit(solution)/shard_map/psum | solution.py:9
  224.4 3.5 %copy-start.7 = (f32[128,512]{1,0:T(8,128)S(1)}, f32[128,512]{1,0:T(8,128)}, u32[]{:S(2)}) copy-start(f32[128,512]{1,0:T(8,128)} %get-tuple-element.118) | copy-start | bytes 786436
  226.6 1.3 copy-start.2
  229.1 107.4 %all-reduce.15.cloned.1.call-start = ((), (), s32[]{:S(2)}) async-start(), calls=%async_computation.3 | async-start | bytes 1048576 | tf_op jit(solution)/shard_map/psum | solution.py:9
  272.2 6.6 %copy-start.5 = (f32[128,512]{1,0:T(8,128)S(1)}, f32[128,512]{1,0:T(8,128)}, u32[]{:S(2)}) copy-start(f32[128,512]{1,0:T(8,128)} %all-reduce.13.cloned.1.call-done) | copy-start | bytes 786436
Sparse Core Ops, SparseCore 0:
  13.2 46.4 all-reduce.18
  64.5 42.9 all-reduce.8
  117.5 54.1 all-reduce.10
  178.0 46.4 all-reduce.16
  229.2 42.9 all-reduce.12
  282.3 54.1 all-reduce.14
where the time goes:
time: 352 us; the launch traced here: 348 us
  waiting for transfers between devices  283 us (80%)
  matrix products  29.4 us (8%)
  between operations  13.9 us (4%)
  other arithmetic  10.7 us (3%)
  local copies, waits for them, and re-layouts  10.2 us (3%)
    psum x4, waiting for transfers between devices, spread(): return lax.psum(kept, axis)  190 us
    psum x2, waiting for transfers between devices, on_device(): lax.psum((swap_taken_rows, swap_top_rows), 'row')  92.6 us
    dot_general x34, matrix products, exact_dot(): jnp.dot(left, right, precision=lax.Precision.HIGHEST, preferred_element_t...  29.4 us
  transfers between devices with their start and end apart: 6, of which 6 were waited for; matrix products, arithmetic and copies ran while one was open for 1% of the time, Pallas kernels for 0%

commit v1 on v0

v1 whole, which is shorter than its diff:
```python
import functools

import jax
import jax.numpy as jnp
from jax import lax
from jax.experimental import pallas as pl
from jax.experimental.pallas import tpu as pltpu
from jax.sharding import PartitionSpec as P

MESH = pl.DeviceIdType.MESH
F32 = jnp.float32
BF16 = jnp.bfloat16
CHUNKS = 8
TILES = 4


def mm(left, right):
    return jnp.dot(left, right, preferred_element_type=F32)


def exact(left, right):
    return jnp.dot(left, right, precision=lax.Precision.HIGHEST, preferred_element_type=F32)


def halves(value):
    high = value.astype(BF16)
    return high, (value - high.astype(F32)).astype(BF16)


def thirds(value):
    high = value.astype(BF16)
    rest = value - high.astype(F32)
    middle = rest.astype(BF16)
    return high, middle, (rest - middle.astype(F32)).astype(BF16)


def select(chosen, value):
    high, middle, low = thirds(value)
    return mm(chosen, high) + (mm(chosen, middle) + mm(chosen, low))


def dot3(left, right):
    left_high, left_low = left
    right_high, right_low = right
    return mm(left_high, right_high) + (mm(left_low, right_high) + mm(left_high, right_low))


def upper_inverse(upper, rows, cols):
    on_diag = rows == cols
    eye = jnp.where(on_diag, 1.0, 0.0)
    kept = jnp.where(on_diag, upper, 0.0)
    scaled = upper / jnp.sum(kept, axis=1, keepdims=True)
    power = jnp.where(rows < cols, -scaled, 0.0)
    result = eye + power
    reach = 2
    while reach < upper.shape[0]:
        power = exact(power, power)
        result = result + exact(result, power)
        reach = reach * 2
    return result / jnp.sum(kept, axis=0, keepdims=True)


def kernel(R, C, nb, a_hbm, piv_ref, linv_ref, out_hbm,
           a_v, asw, sel, sel_t, pm, pf, rsbuf, tops, tp, dpart, dbuf, dh, pan, res,
           u_hi, u_lo, u_f, hit,
           load_sem, out_sem, d_s, d_r, tp_s, tp_r, dh_s, dh_r, rs_s, rs_r, ag_s, ag_r,
           to_s, to_r, ch_s, ch_r, sb_s, sb_r, re_s, re_r):
    height, width = a_v.shape
    two = 2 * nb
    ch = two // R
    ck = height // CHUNKS
    r = lax.axis_index("row")
    c = lax.axis_index("col")
    s = lax.rem(c, 2)
    sibling = {"col": c + 1 - 2 * s}
    half = C // 2

    load = pltpu.make_async_copy(a_hbm, a_v, load_sem)
    load.start()

    barrier = pltpu.get_barrier_semaphore()
    for off in range(1, R):
        pl.semaphore_signal(barrier, inc=1, device_id={"row": lax.rem(r + off, R)}, device_id_type=MESH)
    for off in range(1, half):
        pl.semaphore_signal(barrier, inc=1, device_id={"col": lax.rem(c + 2 * off, C)}, device_id_type=MESH)
    pl.semaphore_signal(barrier, inc=1, device_id=sibling, device_id_type=MESH)

    shift = nb.bit_length() - 1
    rshift = R.bit_length() - 1
    lane = lax.broadcasted_iota(jnp.int32, (nb, nb), 1)
    sub = lax.broadcasted_iota(jnp.int32, (nb, nb), 0)
    for k in range(2):
        p = piv_ref[k:k + 1, :]
        block = jnp.right_shift(p, shift)
        local = jnp.left_shift(jnp.right_shift(block, rshift), shift) + jnp.bitwise_and(p, nb - 1)
        local = jnp.where(jnp.bitwise_and(block, R - 1) == r, local, -1)
        wide = jnp.broadcast_to(local, (nb, nb))
        tall = wide.astype(F32).T
        for t in range(height // nb):
            spots = slice(t * nb, (t + 1) * nb)
            sel[spots, k * nb:(k + 1) * nb] = jnp.where(wide == sub + t * nb, 1.0, 0.0).astype(BF16)
            sel_t[k * nb:(k + 1) * nb, spots] = jnp.where(
                tall == (lane + t * nb).astype(F32), 1.0, 0.0).astype(BF16)

    load.wait()
    pl.semaphore_wait(barrier, R - 1 + half - 1 + 1)

    def remote(src, dst, send, recv, where):
        return pltpu.make_async_remote_copy(
            src_ref=src, dst_ref=dst, send_sem=send, recv_sem=recv, device_id=where, device_id_type=MESH)

    def row_peer(off):
        return {"row": lax.rem(r + off, R)}

    def tp_copy(off):
        q = jnp.minimum(r, 1)
        return remote(a_v.at[0:nb, 0:nb], tp.at[pl.ds(pl.multiple_of(q * nb, nb), nb)],
                      tp_s.at[off - 1], tp_r.at[q], row_peer(off))

    def tops_copy(off):
        q = jnp.minimum(r, 1)
        return remote(a_v.at[0:nb], tops.at[pl.ds(pl.multiple_of(q * nb, nb), nb)],
                      to_s.at[off - 1], to_r.at[q], row_peer(off))

    def d_copy(off):
        return remote(dpart, dbuf.at[off - 1], d_s.at[off - 1], d_r.at[off - 1], row_peer(off))

    def rs_copy(off):
        to = lax.rem(r + off, R)
        return remote(pm.at[pl.ds(pl.multiple_of(to * ch, ch), ch)], rsbuf.at[off - 1],
                      rs_s.at[off - 1], rs_r.at[off - 1], {"row": to})

    def ag_copy(off):
        mine = pf.at[pl.ds(pl.multiple_of(r * ch, ch), ch)]
        return remote(mine, mine, ag_s.at[off - 1], ag_r.at[off - 1], row_peer(off))

    def ag_in(off):
        src = lax.rem(r - off + R, R)
        there = pf.at[pl.ds(pl.multiple_of(src * ch, ch), ch)]
        return remote(there, there, ag_s.at[off - 1], ag_r.at[off - 1], row_peer(off))

    def chain_copy(k):
        part = pan.at[s, pl.ds(k * ck, ck)]
        return remote(part, part, ch_s.at[k], ch_r.at[k], {"col": jnp.minimum(c + 2, C - 2 + s)})

    def sib_copy(k):
        part = pan.at[s, pl.ds(k * ck, ck)]
        return remote(part, part, sb_s.at[k], sb_r.at[k], sibling)

    def sib_in(k):
        part = pan.at[1 - s, pl.ds(k * ck, ck)]
        return remote(part, part, sb_s.at[k], sb_r.at[k], sibling)

    def dh_copy():
        return remote(dh.at[s], dh.at[s], dh_s, dh_r, sibling)

    def dh_in():
        return remote(dh.at[1 - s], dh.at[1 - s], dh_s, dh_r, sibling)

    def res_copy(j, off):
        part = res.at[2 * j:2 * j + 2]
        return remote(part, part, re_s.at[j, off - 1], re_r.at[j], {"col": lax.rem(c + 2 * off, C)})

    is_top = r < 2
    at_root = c < 2

    @pl.when(at_root)
    def _():
        dpart[...] = select(sel_t[...], a_v[:, 0:nb])
        for off in range(1, R):
            d_copy(off).start()

        @pl.when(is_top)
        def _():
            for off in range(1, R):
                tp_copy(off).start()
            tp[pl.ds(pl.multiple_of(jnp.minimum(r, 1) * nb, nb), nb), :] = a_v[0:nb, 0:nb]

    @pl.loop(0, width // nb)
    def _(t):
        spots = pl.ds(pl.multiple_of(t * nb, nb), nb)
        pm[:, spots] = select(sel_t[...], a_v[:, spots])

    for off in range(1, R):
        rs_copy(off).start()

    @pl.when(is_top)
    def _():
        for off in range(1, R):
            tops_copy(off).start()
        tops[pl.ds(pl.multiple_of(jnp.minimum(r, 1) * nb, nb), nb), :] = a_v[0:nb, :]

    ones = jnp.full((two, nb), 1.0, BF16)

    @pl.loop(0, TILES)
    def _(t):
        spots = pl.ds(pl.multiple_of(t * (height // TILES), height // TILES), height // TILES)
        hit[spots, :] = mm(sel[spots, :], ones)

    @pl.when(at_root)
    def _():
        for q in range(2):
            @pl.when(r != q)
            def _():
                part = tp.at[q * nb:(q + 1) * nb]
                remote(part, part, tp_s.at[0], tp_r.at[q], row_peer(1)).wait_recv()
        high, middle, low = thirds(tp[...])
        for k in range(CHUNKS):
            spots = slice(k * ck, (k + 1) * ck)
            chosen = sel[spots, :]
            placed = mm(chosen, high) + (mm(chosen, middle) + mm(chosen, low))
            pan[s, spots, :] = jnp.where(hit[spots, :] > 0.5, placed, a_v[spots, 0:nb])
            chain_copy(k).start()
            sib_copy(k).start()

    @pl.when(at_root)
    def _():
        total = dpart[...]
        for off in range(1, R):
            d_copy(off).wait_recv()
            total = total + dbuf[off - 1]
        dh[s] = total
        dh_copy().start()

    def forward(k):
        @pl.when(c >= 2)
        def _():
            chain_copy(k).wait_recv()

            @pl.when(c + 2 < C)
            def _():
                chain_copy(k).start()
            sib_copy(k).start()

    forward(0)

    own = pl.ds(pl.multiple_of(r * ch, ch), ch)
    total = pm[own, :]
    for off in range(1, R):
        rs_copy(off).wait_recv()
        total = total + rsbuf[off - 1]
    pf[own, :] = total
    for off in range(1, R):
        ag_copy(off).start()

    @pl.when(at_root)
    def _():
        dh_in().wait_recv()
        upper00 = jnp.where(sub <= lane, exact(linv_ref[0], dh[0, 0:nb, :]), 0.0)
        inv0 = upper_inverse(upper00, sub, lane)
        low10 = exact(dh[0, nb:two, :], inv0)
        res[0] = inv0
        res[1] = low10
        for off in range(1, half):
            res_copy(0, off).start()
        upper01 = exact(linv_ref[0], dh[1, 0:nb, :])
        rest = dh[1, nb:two, :] - exact(low10, upper01)
        upper11 = jnp.where(sub <= lane, exact(linv_ref[1], rest), 0.0)
        cross = exact(inv0, upper01)
        inv1 = upper_inverse(upper11, sub, lane)
        res[2] = -exact(cross, inv1)
        res[3] = inv1
        for off in range(1, half):
            res_copy(1, off).start()

    for k in range(1, CHUNKS):
        forward(k)

    for q in range(2):
        @pl.when(r != q)
        def _():
            part = tops.at[q * nb:(q + 1) * nb]
            remote(part, part, to_s.at[0], to_r.at[q], row_peer(1)).wait_recv()

    @pl.loop(0, width // nb)
    def _(t):
        spots = pl.ds(pl.multiple_of(t * nb, nb), nb)
        placed = select(sel[...], tops[:, spots])
        asw[:, spots] = jnp.where(hit[...] > 0.5, placed, a_v[:, spots])

    for off in range(1, R):
        ag_in(off).wait_recv()

    @pl.when(c >= 2)
    def _():
        res_copy(0, 1).wait_recv()
    inv_low0 = linv_ref[0]
    inv_low1 = linv_ref[1]
    mixed = -exact(exact(inv_low1, res[1]), inv_low0)
    u_f[0:nb, :] = dot3(halves(inv_low0), halves(pf[0:nb, :]))
    u_f[nb:two, :] = (dot3(halves(mixed), halves(pf[0:nb, :]))
                      + dot3(halves(inv_low1), halves(pf[nb:two, :])))
    high, low = halves(u_f[...])
    u_hi[...] = high
    u_lo[...] = low

    for k in range(CHUNKS):
        sib_in(k).wait_recv()

    @pl.when(c >= 2)
    def _():
        res_copy(1, 1).wait_recv()

    step = height // TILES
    inv0 = halves(res[0])
    cross = halves(res[2])
    inv1 = halves(res[3])

    def update(t, start):
        spots = pl.ds(start, step)
        left0 = halves(pan[0, spots, :])
        left1 = halves(pan[1, spots, :])
        low0 = dot3(left0, inv0)
        low1 = dot3(left0, cross) + dot3(left1, inv1)
        high, low = halves(jnp.concatenate([low0, low1], axis=1))
        asw[spots, :] = asw[spots, :] - dot3((high, low), (u_hi[...], u_lo[...]))

        @pl.when(c == 0)
        def _():
            asw[spots, 0:nb] = low0

        @pl.when(c == 1)
        def _():
            asw[spots, 0:nb] = low1

    def store(t):
        part = pl.ds(t * step, step)
        return pltpu.make_async_copy(asw.at[part], out_hbm.at[part], out_sem.at[t])

    for t in range(TILES):
        update(t, t * step)
        if t == 0:
            @pl.when(r == 0)
            def _():
                asw[0:nb, :] = u_f[0:nb, :]

                @pl.when(c == 0)
                def _():
                    asw[0:nb, 0:nb] = jnp.where(sub <= lane, u_f[0:nb, 0:nb], 0.0)

            @pl.when(r == 1)
            def _():
                asw[0:nb, :] = u_f[nb:two, :]

                @pl.when(c == 0)
                def _():
                    asw[0:nb, 0:nb] = res[1]

                @pl.when(c == 1)
                def _():
                    asw[0:nb, 0:nb] = jnp.where(sub <= lane, u_f[nb:two, 0:nb], 0.0)
        store(t).start()

    for off in range(1, R):
        rs_copy(off).wait_send()
        ag_copy(off).wait_send()

    @pl.when(is_top)
    def _():
        for off in range(1, R):
            tops_copy(off).wait_send()

        @pl.when(at_root)
        def _():
            for off in range(1, R):
                tp_copy(off).wait_send()

    for k in range(CHUNKS):
        sib_copy(k).wait_send()

        @pl.when(c + 2 < C)
        def _():
            chain_copy(k).wait_send()

    @pl.when(at_root)
    def _():
        dh_copy().wait_send()
        for off in range(1, R):
            d_copy(off).wait_send()
        for off in range(1, half):
            res_copy(0, off).wait_send()
            res_copy(1, off).wait_send()
    for t in range(TILES):
        store(t).wait()


def on_device(matrix, pivots, lower_inverse):
    R = lax.axis_size("row")
    C = lax.axis_size("col")
    height, width = matrix.shape
    nb = lower_inverse.shape[1]
    two = 2 * nb
    dma = pltpu.SemaphoreType.DMA
    vm = pltpu.VMEM
    return pl.pallas_call(
        functools.partial(kernel, R, C, nb),
        out_shape=jax.ShapeDtypeStruct((height, width), F32),
        in_specs=[pl.BlockSpec(memory_space=pl.ANY), pl.BlockSpec(memory_space=pltpu.VMEM),
                  pl.BlockSpec(memory_space=pltpu.VMEM)],
        out_specs=pl.BlockSpec(memory_space=pl.ANY),
        scratch_shapes=[
            vm((height, width), F32), vm((height, width), F32),
            vm((height, two), BF16), vm((two, height), BF16),
            vm((two, width), F32), vm((two, width), F32),
            vm((R - 1, two // R, width), F32), vm((two, width), F32),
            vm((two, nb), F32), vm((two, nb), F32), vm((R - 1, two, nb), F32),
            vm((2, two, nb), F32), vm((2, height, nb), F32), vm((4, nb, nb), F32),
            vm((two, width), BF16), vm((two, width), BF16), vm((two, width), F32),
            vm((height, nb), F32),
            dma, dma((TILES,)), dma((R - 1,)), dma((R - 1,)), dma((R - 1,)), dma((2,)), dma, dma,
            dma((R - 1,)), dma((R - 1,)), dma((R - 1,)), dma((R - 1,)),
            dma((R - 1,)), dma((2,)), dma((CHUNKS,)), dma((CHUNKS,)), dma((CHUNKS,)), dma((CHUNKS,)),
            dma((2, C // 2 - 1)), dma((2,)),
        ],
        compiler_params=pltpu.CompilerParams(
            collective_id=0, has_side_effects=True, vmem_limit_bytes=40 * 1024 * 1024),
    )(matrix, pivots, lower_inverse)


def solution(mesh):
    return jax.shard_map(
        on_device,
        mesh=mesh,
        in_specs=(P("row", "col"), P(), P()),
        out_specs=P("row", "col"),
        check_vma=False,
    )
```

time: 352 us -> 51.9 us (0.15); the launches traced: 348 us -> 51.7 us
  waiting for transfers between devices: 283 us -> 0 us
  Pallas kernels: 0 us -> 47.2 us
  matrix products: 29.4 us -> 0 us
  between operations: 13.9 us -> 0.01 us
  other arithmetic: 10.7 us -> 0 us
  local copies, waits for them, and re-layouts: 10.2 us -> 4.49 us
    psum x6 -> x0, waiting for transfers between devices: 283 us -> none  [the longest x4 190 us: spread(): return lax.psum(kept, axis)]
    pallas_call x0 -> x1, Pallas kernels: none -> 47.2 us  [on_device(): pl.pallas_call(functools.partial(kernel, R, C, nb), out_shape=jax.ShapeDt...]
    dot_general x34 -> x0, matrix products: 29.4 us -> none  [exact_dot(): jnp.dot(left, right, precision=lax.Precision.HIGHEST, preferred_element_t...]
    select_n x5 -> x0, other arithmetic: 5.87 us -> none  [the longest x2 3.47 us: spread(): jnp.where(lax.axis_index(axis) == source, value, 0).astype(value.dtype)]
  transfers between devices with their start and end apart: 6 -> 0, of which waited for: 6 -> 0; matrix products, arithmetic and copies ran while one was open for 1% -> 0% of each run, Pallas kernels for 0% -> 0%
where the time goes in v1:
time: 51.9 us; the launch traced here: 51.7 us
  Pallas kernels  47.2 us (91%)
  local copies, waits for them, and re-layouts  4.49 us (9%)
    pallas_call x1, Pallas kernels, on_device(): pl.pallas_call(functools.partial(kernel, R, C, nb), out_shape=jax.ShapeDt...  47.2 us
    unnamed x7, local copies, waits for them, and re-layouts  4.49 us

profile of v1, /device:TPU:24, one launch (start us, length us, event | category | flops | bytes accessed | tf_op | source)
XLA Modules:
  0.0 51.7 jit_solution(8236159360059463274)
XLA Ops:
  0.0 0.0 copy-start
  0.0 1.6 %copy-done = f32[1024,512]{1,0:T(8,128)S(1)} copy-done((f32[1024,512]{1,0:T(8,128)S(1)}, f32[1024,512]{1,0:T(8,128)}, u32[]{:S(2)}) %copy-start) | copy-done | bytes 2097176
  1.6 0.0 copy-start.1
  1.6 0.9 %copy-done.1 = f32[2,128,128]{2,1,0:T(8,128)S(1)} copy-done((f32[2,128,128]{2,1,0:T(8,128)S(1)}, f32[2,128,128]{2,1,0:T(8,128)}, u32[]{:S(2)}) %copy-start.1) | copy-done | bytes 131096
  2.5 0.0 copy-start.2
  2.5 0.7 %copy-done.2 = s32[2,128]{1,0:T(2,128)S(1)} copy-done((s32[2,128]{1,0:T(2,128)S(1)}, s32[2,128]{1,0:T(2,128)}, u32[]{:S(2)}) %copy-start.2) | copy-done | bytes 1048
  3.2 47.2 %shard_map.37 = f32[1024,512]{1,0:T(8,128)S(1)} custom-call(f32[1024,512]{1,0:T(8,128)S(1)} %copy-done, s32[2,128]{1,0:T(2,128)S(1)} %copy-done.2, f32[2,128,128]{2,1,0:T(8,128)S(1)} %copy-done.1), custom_call_target="tpu_custom_call" | custom-call | tf_op jit(solution)/shard_map/pallas_call | solution.py:395
  50.4 1.3 %copy.5 = f32[1024,512]{1,0:T(8,128)} copy(f32[1024,512]{1,0:T(8,128)S(1)} %shard_map.37) | data formatting | bytes 4194304
Async XLA Ops:
  0.0 1.6 %copy-start = (f32[1024,512]{1,0:T(8,128)S(1)}, f32[1024,512]{1,0:T(8,128)}, u32[]{:S(2)}) copy-start(f32[1024,512]{1,0:T(8,128)} %a_hbm.1) | copy-start | bytes 6291460
  1.6 0.9 %copy-start.1 = (f32[2,128,128]{2,1,0:T(8,128)S(1)}, f32[2,128,128]{2,1,0:T(8,128)}, u32[]{:S(2)}) copy-start(f32[2,128,128]{2,1,0:T(8,128)} %linv_ref.1) | copy-start | bytes 393220
  2.5 0.7 %copy-start.2 = (s32[2,128]{1,0:T(2,128)S(1)}, s32[2,128]{1,0:T(2,128)}, u32[]{:S(2)}) copy-start(s32[2,128]{1,0:T(2,128)} %piv_ref.1) | copy-start | bytes 3076

commit v2 on v1

--- a/solution.py
+++ b/solution.py
@@ -11,6 +11,7 @@
 F32 = jnp.float32
 BF16 = jnp.bfloat16
 CHUNKS = 8
+EARLY = 2
 TILES = 4
 
 
@@ -60,11 +61,11 @@
     return result / jnp.sum(kept, axis=0, keepdims=True)
 
 
-def kernel(R, C, nb, a_hbm, piv_ref, linv_ref, out_hbm,
-           a_v, asw, sel, sel_t, pm, pf, rsbuf, tops, tp, dpart, dbuf, dh, pan, res,
+def kernel(R, C, nb, a_hbm, piv_hbm, linv_hbm, asw,
+           a_v, piv_ref, linv_ref, sel, sel_t, pm, pf, rsbuf, tops, tp, dpart, dbuf, dh, pan, res,
            u_hi, u_lo, u_f, hit,
-           load_sem, out_sem, d_s, d_r, tp_s, tp_r, dh_s, dh_r, rs_s, rs_r, ag_s, ag_r,
-           to_s, to_r, ch_s, ch_r, sb_s, sb_r, re_s, re_r):
+           load_sem, piv_sem, linv_sem, d_s, d_r, tp_s, tp_r, rs_s, rs_r, ag_s, ag_r,
+           to_s, to_r, ch_s, ch_r, sb_s, sb_r):
     height, width = a_v.shape
     two = 2 * nb
     ch = two // R
@@ -73,18 +74,31 @@
     c = lax.axis_index("col")
     s = lax.rem(c, 2)
     sibling = {"col": c + 1 - 2 * s}
-    half = C // 2
 
     load = pltpu.make_async_copy(a_hbm, a_v, load_sem)
+    load_piv = pltpu.make_async_copy(piv_hbm, piv_ref, piv_sem)
+    load_linv = pltpu.make_async_copy(linv_hbm, linv_ref, linv_sem)
+    load_piv.start()
     load.start()
+    load_linv.start()
 
     barrier = pltpu.get_barrier_semaphore()
     for off in range(1, R):
         pl.semaphore_signal(barrier, inc=1, device_id={"row": lax.rem(r + off, R)}, device_id_type=MESH)
-    for off in range(1, half):
-        pl.semaphore_signal(barrier, inc=1, device_id={"col": lax.rem(c + 2 * off, C)}, device_id_type=MESH)
+    has_after = c + 2 < C
+    has_before = c >= 2
+
+    @pl.when(has_after)
+    def _():
+        pl.semaphore_signal(barrier, inc=1, device_id={"col": jnp.minimum(c + 2, C - 1)}, device_id_type=MESH)
+
+    @pl.when(has_before)
+    def _():
+        pl.semaphore_signal(barrier, inc=1, device_id={"col": jnp.maximum(c - 2, 0)}, device_id_type=MESH)
+
     pl.semaphore_signal(barrier, inc=1, device_id=sibling, device_id_type=MESH)
 
+    load_piv.wait()
     shift = nb.bit_length() - 1
     rshift = R.bit_length() - 1
     lane = lax.broadcasted_iota(jnp.int32, (nb, nb), 1)
@@ -103,7 +117,8 @@
                 tall == (lane + t * nb).astype(F32), 1.0, 0.0).astype(BF16)
 
     load.wait()
-    pl.semaphore_wait(barrier, R - 1 + half - 1 + 1)
+    load_linv.wait()
+    pl.semaphore_wait(barrier, R + jnp.minimum(c // 2, 1) + jnp.minimum((C - 1 - c) // 2, 1))
 
     def remote(src, dst, send, recv, where):
         return pltpu.make_async_remote_copy(
@@ -139,27 +154,22 @@
         there = pf.at[pl.ds(pl.multiple_of(src * ch, ch), ch)]
         return remote(there, there, ag_s.at[off - 1], ag_r.at[off - 1], row_peer(off))
 
+    def piece(side, k):
+        if k < CHUNKS:
+            return pan.at[side, pl.ds(k * ck, ck)]
+        return dh.at[side, pl.ds((k - CHUNKS) * nb, nb)]
+
     def chain_copy(k):
-        part = pan.at[s, pl.ds(k * ck, ck)]
+        part = piece(s, k)
         return remote(part, part, ch_s.at[k], ch_r.at[k], {"col": jnp.minimum(c + 2, C - 2 + s)})
 
     def sib_copy(k):
-        part = pan.at[s, pl.ds(k * ck, ck)]
+        part = piece(s, k)
         return remote(part, part, sb_s.at[k], sb_r.at[k], sibling)
 
     def sib_in(k):
-        part = pan.at[1 - s, pl.ds(k * ck, ck)]
+        part = piece(1 - s, k)
         return remote(part, part, sb_s.at[k], sb_r.at[k], sibling)
-
-    def dh_copy():
-        return remote(dh.at[s], dh.at[s], dh_s, dh_r, sibling)
-
-    def dh_in():
-        return remote(dh.at[1 - s], dh.at[1 - s], dh_s, dh_r, sibling)
-
-    def res_copy(j, off):
-        part = res.at[2 * j:2 * j + 2]
-        return remote(part, part, re_s.at[j, off - 1], re_r.at[j], {"col": lax.rem(c + 2 * off, C)})
 
     is_top = r < 2
     at_root = c < 2
@@ -175,20 +185,6 @@
             for off in range(1, R):
                 tp_copy(off).start()
             tp[pl.ds(pl.multiple_of(jnp.minimum(r, 1) * nb, nb), nb), :] = a_v[0:nb, 0:nb]
-
-    @pl.loop(0, width // nb)
-    def _(t):
-        spots = pl.ds(pl.multiple_of(t * nb, nb), nb)
-        pm[:, spots] = select(sel_t[...], a_v[:, spots])
-
-    for off in range(1, R):
-        rs_copy(off).start()
-
-    @pl.when(is_top)
-    def _():
-        for off in range(1, R):
-            tops_copy(off).start()
-        tops[pl.ds(pl.multiple_of(jnp.minimum(r, 1) * nb, nb), nb), :] = a_v[0:nb, :]
 
     ones = jnp.full((two, nb), 1.0, BF16)
 
@@ -197,15 +193,9 @@
         spots = pl.ds(pl.multiple_of(t * (height // TILES), height // TILES), height // TILES)
         hit[spots, :] = mm(sel[spots, :], ones)
 
-    @pl.when(at_root)
-    def _():
-        for q in range(2):
-            @pl.when(r != q)
-            def _():
-                part = tp.at[q * nb:(q + 1) * nb]
-                remote(part, part, tp_s.at[0], tp_r.at[q], row_peer(1)).wait_recv()
+    def panel(first, last):
         high, middle, low = thirds(tp[...])
-        for k in range(CHUNKS):
+        for k in range(first, last):
             spots = slice(k * ck, (k + 1) * ck)
             chosen = sel[spots, :]
             placed = mm(chosen, high) + (mm(chosen, middle) + mm(chosen, low))
@@ -215,12 +205,38 @@
 
     @pl.when(at_root)
     def _():
+        for q in range(2):
+            @pl.when(r != q)
+            def _():
+                part = tp.at[q * nb:(q + 1) * nb]
+                remote(part, part, tp_s.at[0], tp_r.at[q], row_peer(1)).wait_recv()
+        panel(0, EARLY)
+
+    @pl.loop(0, width // nb)
+    def _(t):
+        spots = pl.ds(pl.multiple_of(t * nb, nb), nb)
+        pm[:, spots] = select(sel_t[...], a_v[:, spots])
+
+    for off in range(1, R):
+        rs_copy(off).start()
+
+    @pl.when(is_top)
+    def _():
+        for off in range(1, R):
+            tops_copy(off).start()
+        tops[pl.ds(pl.multiple_of(jnp.minimum(r, 1) * nb, nb), nb), :] = a_v[0:nb, :]
+
+    @pl.when(at_root)
+    def _():
         total = dpart[...]
         for off in range(1, R):
             d_copy(off).wait_recv()
             total = total + dbuf[off - 1]
         dh[s] = total
-        dh_copy().start()
+        for k in range(CHUNKS, CHUNKS + 2):
+            chain_copy(k).start()
+            sib_copy(k).start()
+        panel(EARLY, CHUNKS)
 
     def forward(k):
         @pl.when(c >= 2)
@@ -232,7 +248,10 @@
                 chain_copy(k).start()
             sib_copy(k).start()
 
-    forward(0)
+    for k in range(EARLY):
+        forward(k)
+    forward(CHUNKS)
+    forward(CHUNKS + 1)
 
     own = pl.ds(pl.multiple_of(r * ch, ch), ch)
     total = pm[own, :]
@@ -243,28 +262,28 @@
     for off in range(1, R):
         ag_copy(off).start()
 
-    @pl.when(at_root)
-    def _():
-        dh_in().wait_recv()
-        upper00 = jnp.where(sub <= lane, exact(linv_ref[0], dh[0, 0:nb, :]), 0.0)
-        inv0 = upper_inverse(upper00, sub, lane)
-        low10 = exact(dh[0, nb:two, :], inv0)
-        res[0] = inv0
-        res[1] = low10
-        for off in range(1, half):
-            res_copy(0, off).start()
-        upper01 = exact(linv_ref[0], dh[1, 0:nb, :])
-        rest = dh[1, nb:two, :] - exact(low10, upper01)
-        upper11 = jnp.where(sub <= lane, exact(linv_ref[1], rest), 0.0)
-        cross = exact(inv0, upper01)
-        inv1 = upper_inverse(upper11, sub, lane)
-        res[2] = -exact(cross, inv1)
-        res[3] = inv1
-        for off in range(1, half):
-            res_copy(1, off).start()
-
-    for k in range(1, CHUNKS):
-        forward(k)
+    left = list(range(EARLY, CHUNKS))
+
+    def some(count):
+        for _ in range(min(count, len(left))):
+            forward(left.pop(0))
+
+    sib_in(CHUNKS).wait_recv()
+    sib_in(CHUNKS + 1).wait_recv()
+    upper00 = jnp.where(sub <= lane, exact(linv_ref[0], dh[0, 0:nb, :]), 0.0)
+    res[0] = upper_inverse(upper00, sub, lane)
+    some(2)
+    res[1] = exact(dh[0, nb:two, :], res[0])
+    upper01 = exact(linv_ref[0], dh[1, 0:nb, :])
+    rest = dh[1, nb:two, :] - exact(res[1], upper01)
+    upper11 = jnp.where(sub <= lane, exact(linv_ref[1], rest), 0.0)
+    res[2] = -exact(res[0], upper01)
+    some(2)
+    res[3] = upper_inverse(upper11, sub, lane)
+    some(1)
+    res[2] = exact(res[2], res[3])
+    mixed = -exact(exact(linv_ref[1], res[1]), linv_ref[0])
+    some(CHUNKS)
 
     for q in range(2):
         @pl.when(r != q)
@@ -281,12 +300,8 @@
     for off in range(1, R):
         ag_in(off).wait_recv()
 
-    @pl.when(c >= 2)
-    def _():
-        res_copy(0, 1).wait_recv()
     inv_low0 = linv_ref[0]
     inv_low1 = linv_ref[1]
-    mixed = -exact(exact(inv_low1, res[1]), inv_low0)
     u_f[0:nb, :] = dot3(halves(inv_low0), halves(pf[0:nb, :]))
     u_f[nb:two, :] = (dot3(halves(mixed), halves(pf[0:nb, :]))
                       + dot3(halves(inv_low1), halves(pf[nb:two, :])))
@@ -296,10 +311,6 @@
 
     for k in range(CHUNKS):
         sib_in(k).wait_recv()
-
-    @pl.when(c >= 2)
-    def _():
-        res_copy(1, 1).wait_recv()
 
     step = height // TILES
     inv0 = halves(res[0])
@@ -323,10 +334,6 @@
         def _():
             asw[spots, 0:nb] = low1
 
-    def store(t):
-        part = pl.ds(t * step, step)
-        return pltpu.make_async_copy(asw.at[part], out_hbm.at[part], out_sem.at[t])
-
     for t in range(TILES):
         update(t, t * step)
         if t == 0:
@@ -349,7 +356,6 @@
                 @pl.when(c == 1)
                 def _():
                     asw[0:nb, 0:nb] = jnp.where(sub <= lane, u_f[nb:two, 0:nb], 0.0)
-        store(t).start()
 
     for off in range(1, R):
         rs_copy(off).wait_send()
@@ -365,7 +371,7 @@
             for off in range(1, R):
                 tp_copy(off).wait_send()
 
-    for k in range(CHUNKS):
+    for k in range(CHUNKS + 2):
         sib_copy(k).wait_send()
 
         @pl.when(c + 2 < C)
@@ -374,14 +380,8 @@
 
     @pl.when(at_root)
     def _():
-        dh_copy().wait_send()
         for off in range(1, R):
             d_copy(off).wait_send()
-        for off in range(1, half):
-            res_copy(0, off).wait_send()
-            res_copy(1, off).wait_send()
-    for t in range(TILES):
-        store(t).wait()
 
 
 def on_device(matrix, pivots, lower_inverse):
@@ -395,11 +395,10 @@
     return pl.pallas_call(
         functools.partial(kernel, R, C, nb),
         out_shape=jax.ShapeDtypeStruct((height, width), F32),
-        in_specs=[pl.BlockSpec(memory_space=pl.ANY), pl.BlockSpec(memory_space=pltpu.VMEM),
-                  pl.BlockSpec(memory_space=pltpu.VMEM)],
-        out_specs=pl.BlockSpec(memory_space=pl.ANY),
+        in_specs=[pl.BlockSpec(memory_space=pl.ANY)] * 3,
+        out_specs=pl.BlockSpec(memory_space=pltpu.VMEM),
         scratch_shapes=[
-            vm((height, width), F32), vm((height, width), F32),
+            vm((height, width), F32), vm((2, nb), jnp.int32), vm((2, nb, nb), F32),
             vm((height, two), BF16), vm((two, height), BF16),
             vm((two, width), F32), vm((two, width), F32),
             vm((R - 1, two // R, width), F32), vm((two, width), F32),
@@ -407,13 +406,13 @@
             vm((2, two, nb), F32), vm((2, height, nb), F32), vm((4, nb, nb), F32),
             vm((two, width), BF16), vm((two, width), BF16), vm((two, width), F32),
             vm((height, nb), F32),
-            dma, dma((TILES,)), dma((R - 1,)), dma((R - 1,)), dma((R - 1,)), dma((2,)), dma, dma,
+            dma, dma, dma, dma((R - 1,)), dma((R - 1,)), dma((R - 1,)), dma((2,)),
             dma((R - 1,)), dma((R - 1,)), dma((R - 1,)), dma((R - 1,)),
-            dma((R - 1,)), dma((2,)), dma((CHUNKS,)), dma((CHUNKS,)), dma((CHUNKS,)), dma((CHUNKS,)),
-            dma((2, C // 2 - 1)), dma((2,)),
+            dma((R - 1,)), dma((2,)), dma((CHUNKS + 2,)), dma((CHUNKS + 2,)),
+            dma((CHUNKS + 2,)), dma((CHUNKS + 2,)),
         ],
         compiler_params=pltpu.CompilerParams(
-            collective_id=0, has_side_effects=True, vmem_limit_bytes=40 * 1024 * 1024),
+            collective_id=0, has_side_effects=True, vmem_limit_bytes=61 * 1024 * 1024),
     )(matrix, pivots, lower_inverse)
 
 

time: 51.9 us -> 49.1 us (0.946)
  local copies, waits for them, and re-layouts: 4.49 us -> 3.08 us
  Pallas kernels: 47.2 us -> 45.9 us
    unnamed x7 -> x1, local copies, waits for them, and re-layouts: 4.49 us -> 3.08 us
    pallas_call x1, Pallas kernels: 47.2 us -> 45.9 us  [on_device(): pl.pallas_call(functools.partial(kernel, R, C, nb), out_shape=jax.ShapeDt...]
where the time goes in v2:
time: 49.1 us; the launch traced here: 48.9 us
  Pallas kernels  45.9 us (93%)
  local copies, waits for them, and re-layouts  3.08 us (6%)
    pallas_call x1, Pallas kernels, on_device(): pl.pallas_call(functools.partial(kernel, R, C, nb), out_shape=jax.ShapeDt...  45.9 us
    unnamed x1, local copies, waits for them, and re-layouts  3.08 us

profile of v2, /device:TPU:24, one launch (start us, length us, event | category | flops | bytes accessed | tf_op | source)
XLA Modules:
  0.0 48.9 jit_solution(10139790859860241038)
XLA Ops:
  0.0 45.9 %shard_map.37 = f32[1024,512]{1,0:T(8,128)} custom-call(f32[1024,512]{1,0:T(8,128)} %a_hbm.1, s32[2,128]{1,0:T(2,128)} %piv_hbm.1, f32[2,128,128]{2,1,0:T(8,128)} %linv_hbm.1), custom_call_target="tpu_custom_call" | custom-call | tf_op jit(solution)/shard_map/pallas_call | solution.py:395
  45.9 3.1 %copy.5 = f32[1024,512]{1,0:T(8,128)} copy(f32[1024,512]{1,0:T(8,128)} %shard_map.37) | data formatting | bytes 4194304

commit v3 on v2

--- a/solution.py
+++ b/solution.py
@@ -10,8 +10,8 @@
 MESH = pl.DeviceIdType.MESH
 F32 = jnp.float32
 BF16 = jnp.bfloat16
-CHUNKS = 8
-EARLY = 2
+CHUNKS = 16
+EARLY = 3
 TILES = 4
 
 
@@ -176,15 +176,15 @@
 
     @pl.when(at_root)
     def _():
+        @pl.when(is_top)
+        def _():
+            for off in range(1, R):
+                tp_copy(off).start()
+            tp[pl.ds(pl.multiple_of(jnp.minimum(r, 1) * nb, nb), nb), :] = a_v[0:nb, 0:nb]
+
         dpart[...] = select(sel_t[...], a_v[:, 0:nb])
         for off in range(1, R):
             d_copy(off).start()
-
-        @pl.when(is_top)
-        def _():
-            for off in range(1, R):
-                tp_copy(off).start()
-            tp[pl.ds(pl.multiple_of(jnp.minimum(r, 1) * nb, nb), nb), :] = a_v[0:nb, 0:nb]
 
     ones = jnp.full((two, nb), 1.0, BF16)
 
@@ -272,18 +272,18 @@
     sib_in(CHUNKS + 1).wait_recv()
     upper00 = jnp.where(sub <= lane, exact(linv_ref[0], dh[0, 0:nb, :]), 0.0)
     res[0] = upper_inverse(upper00, sub, lane)
-    some(2)
+    some(1)
     res[1] = exact(dh[0, nb:two, :], res[0])
     upper01 = exact(linv_ref[0], dh[1, 0:nb, :])
     rest = dh[1, nb:two, :] - exact(res[1], upper01)
     upper11 = jnp.where(sub <= lane, exact(linv_ref[1], rest), 0.0)
     res[2] = -exact(res[0], upper01)
+    some(1)
+    res[3] = upper_inverse(upper11, sub, lane)
     some(2)
-    res[3] = upper_inverse(upper11, sub, lane)
-    some(1)
     res[2] = exact(res[2], res[3])
     mixed = -exact(exact(linv_ref[1], res[1]), linv_ref[0])
-    some(CHUNKS)
+    some(1)
 
     for q in range(2):
         @pl.when(r != q)
@@ -291,11 +291,11 @@
             part = tops.at[q * nb:(q + 1) * nb]
             remote(part, part, to_s.at[0], to_r.at[q], row_peer(1)).wait_recv()
 
-    @pl.loop(0, width // nb)
-    def _(t):
-        spots = pl.ds(pl.multiple_of(t * nb, nb), nb)
+    for t in range(width // nb):
+        spots = slice(t * nb, (t + 1) * nb)
         placed = select(sel[...], tops[:, spots])
         asw[:, spots] = jnp.where(hit[...] > 0.5, placed, a_v[:, spots])
+        some(1)
 
     for off in range(1, R):
         ag_in(off).wait_recv()
@@ -309,9 +309,6 @@
     u_hi[...] = high
     u_lo[...] = low
 
-    for k in range(CHUNKS):
-        sib_in(k).wait_recv()
-
     step = height // TILES
     inv0 = halves(res[0])
     cross = halves(res[2])
@@ -334,7 +331,13 @@
         def _():
             asw[spots, 0:nb] = low1
 
+    per_tile = CHUNKS // TILES
     for t in range(TILES):
+        some(1)
+        while left and left[0] < (t + 1) * per_tile:
+            some(1)
+        for k in range(t * per_tile, (t + 1) * per_tile):
+            sib_in(k).wait_recv()
         update(t, t * step)
         if t == 0:
             @pl.when(r == 0)
@@ -412,7 +415,7 @@
             dma((CHUNKS + 2,)), dma((CHUNKS + 2,)),
         ],
         compiler_params=pltpu.CompilerParams(
-            collective_id=0, has_side_effects=True, vmem_limit_bytes=61 * 1024 * 1024),
+            collective_id=0, has_side_effects=True, vmem_limit_bytes=56 * 1024 * 1024),
     )(matrix, pivots, lower_inverse)
 
 

time: 49.1 us -> 46.7 us (0.951)
  the two profiles are of different devices: /device:TPU:24 before, /device:TPU:29 now
where the time goes in v3:
time: 46.7 us; the launch traced here: 46.5 us
  Pallas kernels  43.4 us (93%)
  local copies, waits for them, and re-layouts  3.08 us (7%)
    pallas_call x1, Pallas kernels, on_device(): pl.pallas_call(functools.partial(kernel, R, C, nb), out_shape=jax.ShapeDt...  43.4 us
    unnamed x1, local copies, waits for them, and re-layouts  3.08 us

profile of v3, /device:TPU:29, one launch (start us, length us, event | category | flops | bytes accessed | tf_op | source)
XLA Modules:
  0.0 46.5 jit_solution(932211109132473440)
XLA Ops:
  0.0 43.4 %shard_map.37 = f32[1024,512]{1,0:T(8,128)} custom-call(f32[1024,512]{1,0:T(8,128)} %a_hbm.1, s32[2,128]{1,0:T(2,128)} %piv_hbm.1, f32[2,128,128]{2,1,0:T(8,128)} %linv_hbm.1), custom_call_target="tpu_custom_call" | custom-call | tf_op jit(solution)/shard_map/pallas_call | solution.py:398
  43.4 3.1 %copy.5 = f32[1024,512]{1,0:T(8,128)} copy(f32[1024,512]{1,0:T(8,128)} %shard_map.37) | data formatting | bytes 4194304

commit v4 on v3

--- a/solution.py
+++ b/solution.py
@@ -203,6 +203,11 @@
             chain_copy(k).start()
             sib_copy(k).start()
 
+    @pl.loop(0, width // nb)
+    def _(t):
+        spots = pl.ds(pl.multiple_of(t * nb, nb), nb)
+        pm[:, spots] = select(sel_t[...], a_v[:, spots])
+
     @pl.when(at_root)
     def _():
         for q in range(2):
@@ -211,11 +216,6 @@
                 part = tp.at[q * nb:(q + 1) * nb]
                 remote(part, part, tp_s.at[0], tp_r.at[q], row_peer(1)).wait_recv()
         panel(0, EARLY)
-
-    @pl.loop(0, width // nb)
-    def _(t):
-        spots = pl.ds(pl.multiple_of(t * nb, nb), nb)
-        pm[:, spots] = select(sel_t[...], a_v[:, spots])
 
     for off in range(1, R):
         rs_copy(off).start()

time: 46.7 us -> 46.7 us (level)
  no operation moved by 1% of the time
where the time goes in v4:
time: 46.7 us; the launch traced here: 46.5 us
  Pallas kernels  43.4 us (93%)
  local copies, waits for them, and re-layouts  3.08 us (7%)
    pallas_call x1, Pallas kernels, on_device(): pl.pallas_call(functools.partial(kernel, R, C, nb), out_shape=jax.ShapeDt...  43.4 us
    unnamed x1, local copies, waits for them, and re-layouts  3.08 us

profile of v4, /device:TPU:29, one launch (start us, length us, event | category | flops | bytes accessed | tf_op | source)
XLA Modules:
  0.0 46.5 jit_solution(17943831885602585884)
XLA Ops:
  0.0 43.4 %shard_map.37 = f32[1024,512]{1,0:T(8,128)} custom-call(f32[1024,512]{1,0:T(8,128)} %a_hbm.1, s32[2,128]{1,0:T(2,128)} %piv_hbm.1, f32[2,128,128]{2,1,0:T(8,128)} %linv_hbm.1), custom_call_target="tpu_custom_call" | custom-call | tf_op jit(solution)/shard_map/pallas_call | solution.py:398
  43.4 3.1 %copy.5 = f32[1024,512]{1,0:T(8,128)} copy(f32[1024,512]{1,0:T(8,128)} %shard_map.37) | data formatting | bytes 4194304
